TPU v7x, 256 devices: a whole 4x4x8 slice. The times are simulated.
256 devices in a mesh: segment: 16 (over x_lo, z), tp: 16 (over y, x_hi, core).
Axes of the slice: x: 4 (x_hi: 2, x_lo: 2; x = x_hi * 2 + x_lo), y: 4, z: 8, core: 2. Of those that a mesh axis runs over, the one named last changes fastest.
Arguments:
- layer_inputs: bfloat16 [16, 2, 128, 2048], P('segment', None, 'tp'), may hold values from -100 to 100, as said below
- cotangent: bfloat16 [2, 2, 128, 2048], P(None, None, 'tp'), may hold values from -6 to 6
- gate_weight: bfloat16 [16, 2048, 4096], P('segment', None, 'tp'), may hold values from -1 to 1, as said below
- up_weight: bfloat16 [16, 2048, 4096], P('segment', None, 'tp'), may hold values from -1 to 1, as said below
- down_weight: bfloat16 [16, 4096, 2048], P('segment', 'tp'), may hold values from -1 to 1, as said below
- gate_momentum: float32 [16, 1024, 4096], P('segment', None, 'tp'), may hold values from -48 to 48
- up_momentum: float32 [16, 1024, 4096], P('segment', None, 'tp'), may hold values from -48 to 48
- down_momentum: float32 [16, 4096, 1024], P('segment', 'tp'), may hold values from -48 to 48
Outputs:
- input_gradient: bfloat16 [16, 2, 128, 2048], P('segment', None, 'tp')
- new_gate_momentum: float32 [16, 1024, 4096], P('segment', None, 'tp')
- new_up_momentum: float32 [16, 1024, 4096], P('segment', None, 'tp')
- new_down_momentum: float32 [16, 4096, 1024], P('segment', 'tp')
Inputs may be any that keep to these rules, and one draw needn't show every extreme that they name: `layer_inputs`: stored layer inputs, independent for every section and micro-batch. `gate_weight`: sections 2l and 2l + 1 hold equal copies of one layer's weights. `up_weight`: sections 2l and 2l + 1 hold equal copies of one layer's weights. `down_weight`: sections 2l and 2l + 1 hold equal copies of one layer's weights.
All inputs are finite; a program needn't handle non-finite values.
Results may differ from a plain program's by a relative error of at most 0.02.
Values may be sent and summed in bfloat16 or wider, within the bound.
No kernel may reach another device: no remote copies, remote signals or barrier semaphores. Data moves between devices by JAX's collectives and lax.ppermute only.
A program may use at most 64 MiB of HBM per device.

v0:
```python
import jax
import jax.numpy as jnp
from jax import lax
from jax.sharding import PartitionSpec as P

epsilon = 1e-05
momentum_decay = 0.9


def passed_along(block, axis, distance):
    devices = range(lax.axis_size(axis))
    route = [(i - distance, i) for i in devices if i - distance in devices]
    return lax.ppermute(block, axis, route)


def partner(block, axis, distance):
    count = lax.axis_size(axis)
    route = []
    for low in range(count):
        high = low | 1 << distance
        if high != low and high < count:
            route += [(low, high), (high, low)]
    return lax.ppermute(block, axis, route)


def contract_last(left, right):
    return lax.dot_general(
        left, right, (((1,), (1,)), ((), ())), preferred_element_type=jnp.float32
    )


def contract_rows(left, right):
    return lax.dot_general(
        left, right, (((0,), (0,)), ((), ())), preferred_element_type=jnp.float32
    )


def project(rows, gate_w, up_w):
    gate = jnp.dot(rows, gate_w, preferred_element_type=jnp.float32)
    up = jnp.dot(rows, up_w, preferred_element_type=jnp.float32)
    return (gate, up)


def backward_factors(incoming_rows, gate, up, down_w):
    hidden_grad = contract_last(incoming_rows, down_w)
    sigma = jax.nn.sigmoid(gate)
    silu = gate * sigma
    hidden = (silu * up).astype(jnp.bfloat16)
    gate_grad = (hidden_grad * up * sigma * (1.0 + gate * (1.0 - sigma))).astype(jnp.bfloat16)
    up_grad = (hidden_grad * silu).astype(jnp.bfloat16)
    return (hidden, gate_grad, up_grad)


def owned(array, start, size, axis):
    return lax.dynamic_slice_in_dim(array, start, size, axis)


def shards(
    layer_inputs,
    cotangent,
    gate_weight,
    up_weight,
    down_weight,
    gate_momentum,
    up_momentum,
    down_momentum,
):
    segments = lax.axis_size("segment")
    depth = segments // 2
    segment = lax.axis_index("segment")
    direction = segment % 2
    lower = direction == 0
    position = segment // 2
    gate_w = gate_weight[0]
    up_w = up_weight[0]
    down_w = down_weight[0]
    inputs = layer_inputs[0].astype(jnp.float32)
    micro, rows_dev, width = inputs.shape
    half = width // 2
    hidden_dev = gate_w.shape[1]
    total_rows = rows_dev * lax.axis_size("tp")
    inverse_norm = lax.rsqrt(jnp.mean(inputs * inputs, axis=-1, keepdims=True) + epsilon)
    exact = inputs * inverse_norm
    normed = exact.astype(jnp.bfloat16)
    entry = lax.dynamic_index_in_dim(cotangent, direction, 0, keepdims=False)
    ticks = depth + micro - 1
    extra = (
        jnp.zeros((width, hidden_dev), jnp.float32),
        jnp.zeros((width, hidden_dev), jnp.float32),
        jnp.zeros((hidden_dev, width), jnp.float32),
    )

    def process(tick, received, state):
        outgoing, backs, extra = state
        index = tick - position
        active = (index >= 0) & (index < micro)
        slot = jnp.clip(index, 0, micro - 1)
        local_in = jnp.where(position == 0, entry[slot], received)
        incoming_rows = lax.all_gather(local_in, "tp", axis=0, tiled=True)
        full_rows = lax.all_gather(normed[slot], "tp", axis=0, tiled=True)

        def factors():
            gate, up = project(full_rows, gate_w, up_w)
            return backward_factors(incoming_rows, gate, up, down_w)

        def resting():
            blank = jnp.zeros((total_rows, hidden_dev), jnp.bfloat16)
            return (blank, blank, blank)

        hidden, gate_grad, up_grad = lax.cond(active, factors, resting)
        count = lax.axis_size("tp") * rows_dev

        def compute():
            return contract_last(gate_grad, gate_w) + contract_last(up_grad, up_w)

        def quiet():
            return jnp.zeros((count, width), jnp.float32)

        normed_grad = lax.psum_scatter(
            lax.cond(active, compute, quiet).astype(jnp.bfloat16),
            "tp",
            scatter_dimension=0,
            tiled=True,
        ).astype(jnp.float32)
        scale = inverse_norm[slot]
        base = exact[slot]
        back = local_in.astype(jnp.float32) + scale * (
            normed_grad - base * jnp.mean(normed_grad * base, axis=-1, keepdims=True)
        )
        back = back.astype(jnp.bfloat16)
        backs = lax.dynamic_update_index_in_dim(
            backs, jnp.where(active, back, backs[slot]), slot, 0
        )

        def accumulate(totals):
            return (
                totals[0] + contract_rows(full_rows, gate_grad),
                totals[1] + contract_rows(full_rows, up_grad),
                totals[2] + contract_rows(hidden, incoming_rows),
            )

        def unchanged(totals):
            return totals

        extra = lax.cond(active, accumulate, unchanged, extra)
        return (back, backs, extra)

    zero_rows = jnp.zeros((rows_dev, width), jnp.bfloat16)
    state = process(
        0, zero_rows, (zero_rows, jnp.zeros((micro, rows_dev, width), jnp.bfloat16), extra)
    )

    def advance(tick, state):
        received = passed_along(state[0], "segment", 2)
        return process(tick, received, state)

    outgoing, backs, extra = lax.fori_loop(1, ticks, advance, state)
    keep_start = jnp.where(lower, 0, half)
    send_start = half - keep_start
    gate_total, up_total, down_total = extra
    arrived = partner(
        (
            owned(gate_total, send_start, half, 0).astype(jnp.bfloat16),
            owned(up_total, send_start, half, 0).astype(jnp.bfloat16),
            owned(down_total, send_start, half, 1).astype(jnp.bfloat16),
        ),
        "segment",
        0,
    )
    gate_share = owned(gate_total, keep_start, half, 0) + arrived[0].astype(jnp.float32)
    up_share = owned(up_total, keep_start, half, 0) + arrived[1].astype(jnp.float32)
    down_share = owned(down_total, keep_start, half, 1) + arrived[2].astype(jnp.float32)
    new_gate = (momentum_decay * gate_momentum[0] + gate_share)[None]
    new_up = (momentum_decay * up_momentum[0] + up_share)[None]
    new_down = (momentum_decay * down_momentum[0] + down_share)[None]
    return (backs[None], new_gate, new_up, new_down)


def solution(mesh):
    return jax.shard_map(
        shards,
        mesh=mesh,
        in_specs=(
            P("segment", None, "tp", None),
            P(None, None, "tp", None),
            P("segment", None, "tp"),
            P("segment", None, "tp"),
            P("segment", "tp", None),
            P("segment", None, "tp"),
            P("segment", None, "tp"),
            P("segment", "tp", None),
        ),
        out_specs=(
            P("segment", None, "tp", None),
            P("segment", None, "tp"),
            P("segment", None, "tp"),
            P("segment", "tp", None),
        ),
        check_vma=False,
    )
```

profile of v0, /device:TPU:32, one launch (start us, length us, event | category | flops | bytes accessed | tf_op | source)
XLA Modules:
  0.0 1206.1 jit_solution(18428818250983817290)
XLA Ops:
  10.5 26.7 %all-gather.1 = bf16[1,128,2048]{2,1,0:T(8,128)(2,1)S(1)} all-gather(bf16[1,8,2048]{2,1,0:T(8,128)(2,1)S(1)} %constant_dynamic-slice_fusion.3), channel_id=3, replica_groups=mesh['segment'=16,'tp'=16] {'tp'}, dimensions={1}, use_global_device_ids=true | all-gather | bytes 557056 | tf_op jit(solution)/shard_map/all_gather | solution.py:100
  38.0 23.0 %all-gather.2 = bf16[1,1,128,2048]{3,2,1,0:T(8,128)(2,1)} all-gather(bf16[1,1,8,2048]{3,2,1,0:T(8,128)(2,1)S(1)} %dynamic-slice_select_fusion), channel_id=4, replica_groups=mesh['segment'=16,'tp'=16] {'tp'}, dimensions={2}, use_global_device_ids=true | all-gather | bytes 557056 | tf_op jit(solution)/shard_map/all_gather | solution.py:99
  76.0 60.9 %reduce-scatter.3.cloned.1.call-done = bf16[8,2048]{1,0:T(8,128)(2,1)} async-done(((bf16[128,2048]{1,0:T(8,128)(2,1)}), bf16[8,2048]{1,0:T(8,128)(2,1)}) %reduce-scatter.3.cloned.1.call-update) | async-done | bytes 32784 | tf_op jit(solution)/shard_map/reduce_scatter | solution.py:119
  139.9 1021.5 %while.22 = (s32[]{:T(128)}, bf16[8,2048]{1,0:T(8,128)(2,1)}, bf16[2,8,2048]{2,1,0:T(8,128)(2,1)}, f32[2048,256]{1,0:T(8,128)}, f32[2048,256]{1,0:T(8,128)}, /*i...) while((s32[]{:T(128)}, bf16[8,2048]{1,0:T(8,128)(2,1)}, ...), condition=%wide.region_18.19_spmd, body=%wide.region_9.18_spmd.sunk | while | flops 1076527104 | bytes 32310056 | solution.py:157
  145.1 23.9 %all-gather.4 = bf16[1,128,2048]{2,1,0:T(8,128)(2,1)S(1)} all-gather(bf16[1,8,2048]{2,1,0:T(8,128)(2,1)S(1)} %constant_dynamic-slice_fusion.8), channel_id=2, replica_groups=mesh['segment'=16,'tp'=16] {'tp'}, dimensions={1}, use_global_device_ids=true | all-gather | bytes 557056 | tf_op jit(solution)/shard_map/while/body/eval_jaxpr/all_gather | solution.py:100
  206.3 59.0 %reduce-scatter.5.cloned.1.call-done = bf16[8,2048]{1,0:T(8,128)(2,1)} async-done(((bf16[128,2048]{1,0:T(8,128)(2,1)}), bf16[8,2048]{1,0:T(8,128)(2,1)}) %reduce-scatter.5.cloned.1.call-update) | async-done | bytes 32784 | tf_op jit(solution)/shard_map/while/body/eval_jaxpr/reduce_scatter | solution.py:119
  272.9 23.8 %all-gather.4 = bf16[1,128,2048]{2,1,0:T(8,128)(2,1)S(1)} all-gather(bf16[1,8,2048]{2,1,0:T(8,128)(2,1)S(1)} %constant_dynamic-slice_fusion.8), channel_id=2, replica_groups=mesh['segment'=16,'tp'=16] {'tp'}, dimensions={1}, use_global_device_ids=true | all-gather | bytes 557056 | tf_op jit(solution)/shard_map/while/body/eval_jaxpr/all_gather | solution.py:100
  297.5 22.1 %all_gather.25 = bf16[128,2048]{1,0:T(8,128)(2,1)S(1)} all-gather(bf16[8,2048]{1,0:T(8,128)(2,1)S(1)} %bitcast_select_fusion.3), channel_id=1, replica_groups=mesh['segment'=16,'tp'=16] {'tp'}, dimensions={0}, use_global_device_ids=true | all-gather | bytes 557056 | tf_op jit(solution)/shard_map/while/body/eval_jaxpr/all_gather | solution.py:99
  321.4 71.9 %reduce-scatter.5.cloned.1.call-done = bf16[8,2048]{1,0:T(8,128)(2,1)} async-done(((bf16[128,2048]{1,0:T(8,128)(2,1)}), bf16[8,2048]{1,0:T(8,128)(2,1)}) %reduce-scatter.5.cloned.1.call-update) | async-done | bytes 32784 | tf_op jit(solution)/shard_map/while/body/eval_jaxpr/reduce_scatter | solution.py:119
  400.8 23.8 %all-gather.4 = bf16[1,128,2048]{2,1,0:T(8,128)(2,1)S(1)} all-gather(bf16[1,8,2048]{2,1,0:T(8,128)(2,1)S(1)} %constant_dynamic-slice_fusion.8), channel_id=2, replica_groups=mesh['segment'=16,'tp'=16] {'tp'}, dimensions={1}, use_global_device_ids=true | all-gather | bytes 557056 | tf_op jit(solution)/shard_map/while/body/eval_jaxpr/all_gather | solution.py:100
  425.4 22.1 %all_gather.25 = bf16[128,2048]{1,0:T(8,128)(2,1)S(1)} all-gather(bf16[8,2048]{1,0:T(8,128)(2,1)S(1)} %bitcast_select_fusion.3), channel_id=1, replica_groups=mesh['segment'=16,'tp'=16] {'tp'}, dimensions={0}, use_global_device_ids=true | all-gather | bytes 557056 | tf_op jit(solution)/shard_map/while/body/eval_jaxpr/all_gather | solution.py:99
  449.3 71.9 %reduce-scatter.5.cloned.1.call-done = bf16[8,2048]{1,0:T(8,128)(2,1)} async-done(((bf16[128,2048]{1,0:T(8,128)(2,1)}), bf16[8,2048]{1,0:T(8,128)(2,1)}) %reduce-scatter.5.cloned.1.call-update) | async-done | bytes 32784 | tf_op jit(solution)/shard_map/while/body/eval_jaxpr/reduce_scatter | solution.py:119
  528.7 23.8 %all-gather.4 = bf16[1,128,2048]{2,1,0:T(8,128)(2,1)S(1)} all-gather(bf16[1,8,2048]{2,1,0:T(8,128)(2,1)S(1)} %constant_dynamic-slice_fusion.8), channel_id=2, replica_groups=mesh['segment'=16,'tp'=16] {'tp'}, dimensions={1}, use_global_device_ids=true | all-gather | bytes 557056 | tf_op jit(solution)/shard_map/while/body/eval_jaxpr/all_gather | solution.py:100
  577.2 71.1 %reduce-scatter.5.cloned.1.call-done = bf16[8,2048]{1,0:T(8,128)(2,1)} async-done(((bf16[128,2048]{1,0:T(8,128)(2,1)}), bf16[8,2048]{1,0:T(8,128)(2,1)}) %reduce-scatter.5.cloned.1.call-update) | async-done | bytes 32784 | tf_op jit(solution)/shard_map/while/body/eval_jaxpr/reduce_scatter | solution.py:119
  655.9 23.8 %all-gather.4 = bf16[1,128,2048]{2,1,0:T(8,128)(2,1)S(1)} all-gather(bf16[1,8,2048]{2,1,0:T(8,128)(2,1)S(1)} %constant_dynamic-slice_fusion.8), channel_id=2, replica_groups=mesh['segment'=16,'tp'=16] {'tp'}, dimensions={1}, use_global_device_ids=true | all-gather | bytes 557056 | tf_op jit(solution)/shard_map/while/body/eval_jaxpr/all_gather | solution.py:100
  704.3 72.2 %reduce-scatter.5.cloned.1.call-done = bf16[8,2048]{1,0:T(8,128)(2,1)} async-done(((bf16[128,2048]{1,0:T(8,128)(2,1)}), bf16[8,2048]{1,0:T(8,128)(2,1)}) %reduce-scatter.5.cloned.1.call-update) | async-done | bytes 32784 | tf_op jit(solution)/shard_map/while/body/eval_jaxpr/reduce_scatter | solution.py:119
  784.1 23.8 %all-gather.4 = bf16[1,128,2048]{2,1,0:T(8,128)(2,1)S(1)} all-gather(bf16[1,8,2048]{2,1,0:T(8,128)(2,1)S(1)} %constant_dynamic-slice_fusion.8), channel_id=2, replica_groups=mesh['segment'=16,'tp'=16] {'tp'}, dimensions={1}, use_global_device_ids=true | all-gather | bytes 557056 | tf_op jit(solution)/shard_map/while/body/eval_jaxpr/all_gather | solution.py:100
  808.7 22.1 %all_gather.25 = bf16[128,2048]{1,0:T(8,128)(2,1)S(1)} all-gather(bf16[8,2048]{1,0:T(8,128)(2,1)S(1)} %bitcast_select_fusion.3), channel_id=1, replica_groups=mesh['segment'=16,'tp'=16] {'tp'}, dimensions={0}, use_global_device_ids=true | all-gather | bytes 557056 | tf_op jit(solution)/shard_map/while/body/eval_jaxpr/all_gather | solution.py:99
  832.6 72.3 %reduce-scatter.5.cloned.1.call-done = bf16[8,2048]{1,0:T(8,128)(2,1)} async-done(((bf16[128,2048]{1,0:T(8,128)(2,1)}), bf16[8,2048]{1,0:T(8,128)(2,1)}) %reduce-scatter.5.cloned.1.call-update) | async-done | bytes 32784 | tf_op jit(solution)/shard_map/while/body/eval_jaxpr/reduce_scatter | solution.py:119
  912.5 23.9 %all-gather.4 = bf16[1,128,2048]{2,1,0:T(8,128)(2,1)S(1)} all-gather(bf16[1,8,2048]{2,1,0:T(8,128)(2,1)S(1)} %constant_dynamic-slice_fusion.8), channel_id=2, replica_groups=mesh['segment'=16,'tp'=16] {'tp'}, dimensions={1}, use_global_device_ids=true | all-gather | bytes 557056 | tf_op jit(solution)/shard_map/while/body/eval_jaxpr/all_gather | solution.py:100
  960.9 72.4 %reduce-scatter.5.cloned.1.call-done = bf16[8,2048]{1,0:T(8,128)(2,1)} async-done(((bf16[128,2048]{1,0:T(8,128)(2,1)}), bf16[8,2048]{1,0:T(8,128)(2,1)}) %reduce-scatter.5.cloned.1.call-update) | async-done | bytes 32784 | tf_op jit(solution)/shard_map/while/body/eval_jaxpr/reduce_scatter | solution.py:119
  1040.9 23.8 %all-gather.4 = bf16[1,128,2048]{2,1,0:T(8,128)(2,1)S(1)} all-gather(bf16[1,8,2048]{2,1,0:T(8,128)(2,1)S(1)} %constant_dynamic-slice_fusion.8), channel_id=2, replica_groups=mesh['segment'=16,'tp'=16] {'tp'}, dimensions={1}, use_global_device_ids=true | all-gather | bytes 557056 | tf_op jit(solution)/shard_map/while/body/eval_jaxpr/all_gather | solution.py:100
  1065.5 22.1 %all_gather.25 = bf16[128,2048]{1,0:T(8,128)(2,1)S(1)} all-gather(bf16[8,2048]{1,0:T(8,128)(2,1)S(1)} %bitcast_select_fusion.3), channel_id=1, replica_groups=mesh['segment'=16,'tp'=16] {'tp'}, dimensions={0}, use_global_device_ids=true | all-gather | bytes 557056 | tf_op jit(solution)/shard_map/while/body/eval_jaxpr/all_gather | solution.py:99
  1089.3 69.7 %reduce-scatter.5.cloned.1.call-done = bf16[8,2048]{1,0:T(8,128)(2,1)} async-done(((bf16[128,2048]{1,0:T(8,128)(2,1)}), bf16[8,2048]{1,0:T(8,128)(2,1)}) %reduce-scatter.5.cloned.1.call-update) | async-done | bytes 32784 | tf_op jit(solution)/shard_map/while/body/eval_jaxpr/reduce_scatter | solution.py:119
  (210 shorter events, 274.7 us)
Async XLA Ops:
  7.2 129.7 %reduce-scatter.3.cloned.1.call-start = ((), (), s32[]{:S(2)}) async-start(), calls=%async_computation.2 | async-start | bytes 557056 | tf_op jit(solution)/shard_map/reduce_scatter | solution.py:119
  68.9 71.0 %copy-start = (bf16[1,2048,256]{2,1,0:T(8,128)(2,1)S(1)}, bf16[1,2048,256]{2,1,0:T(8,128)(2,1)}, u32[]{:S(2)}) copy-start(bf16[1,2048,256]{2,1,0:T(8,128)(2,1)} %param.24) | copy-start | bytes 3145732
  68.9 71.0 %copy-start.1 = (bf16[1,2048,256]{2,1,0:T(8,128)(2,1)S(1)}, bf16[1,2048,256]{2,1,0:T(8,128)(2,1)}, u32[]{:S(2)}) copy-start(bf16[1,2048,256]{2,1,0:T(8,128)(2,1)} %param.25) | copy-start | bytes 3145732
  139.9 125.5 %reduce-scatter.5.cloned.1.call-start = ((), (), s32[]{:S(2)}) async-start(), calls=%async_computation.3 | async-start | bytes 557056 | tf_op jit(solution)/shard_map/while/body/eval_jaxpr/reduce_scatter | solution.py:119
  139.9 29.1 %collective-permute-start = (bf16[8,2048]{1,0:T(8,128)(2,1)}, bf16[8,2048]{1,0:T(8,128)(2,1)S(1)}, u32[]{:S(2)}, u32[]{:S(2)}) collective-permute-start(bf16[8,2048]{1,0:T(8,128)(2,1)} %get-tuple-element.645), channel_id=1, source_target_pairs={{0,32},{16,48},{32,64},{48,80},{64,96},{80,112},{96,128},{112,144}... | collective-permute-start | bytes 98312 | tf_op jit(solution)/shard_map/while/body/eval_jaxpr/ppermute | solution.py:13
  267.7 125.5 %reduce-scatter.5.cloned.1.call-start = ((), (), s32[]{:S(2)}) async-start(), calls=%async_computation.3 | async-start | bytes 557056 | tf_op jit(solution)/shard_map/while/body/eval_jaxpr/reduce_scatter | solution.py:119
  267.7 29.1 %collective-permute-start = (bf16[8,2048]{1,0:T(8,128)(2,1)}, bf16[8,2048]{1,0:T(8,128)(2,1)S(1)}, u32[]{:S(2)}, u32[]{:S(2)}) collective-permute-start(bf16[8,2048]{1,0:T(8,128)(2,1)} %get-tuple-element.645), channel_id=1, source_target_pairs={{0,32},{16,48},{32,64},{48,80},{64,96},{80,112},{96,128},{112,144}... | collective-permute-start | bytes 98312 | tf_op jit(solution)/shard_map/while/body/eval_jaxpr/ppermute | solution.py:13
  395.6 125.5 %reduce-scatter.5.cloned.1.call-start = ((), (), s32[]{:S(2)}) async-start(), calls=%async_computation.3 | async-start | bytes 557056 | tf_op jit(solution)/shard_map/while/body/eval_jaxpr/reduce_scatter | solution.py:119
  395.6 29.1 %collective-permute-start = (bf16[8,2048]{1,0:T(8,128)(2,1)}, bf16[8,2048]{1,0:T(8,128)(2,1)S(1)}, u32[]{:S(2)}, u32[]{:S(2)}) collective-permute-start(bf16[8,2048]{1,0:T(8,128)(2,1)} %get-tuple-element.645), channel_id=1, source_target_pairs={{0,32},{16,48},{32,64},{48,80},{64,96},{80,112},{96,128},{112,144}... | collective-permute-start | bytes 98312 | tf_op jit(solution)/shard_map/while/body/eval_jaxpr/ppermute | solution.py:13
  523.5 124.7 %reduce-scatter.5.cloned.1.call-start = ((), (), s32[]{:S(2)}) async-start(), calls=%async_computation.3 | async-start | bytes 557056 | tf_op jit(solution)/shard_map/while/body/eval_jaxpr/reduce_scatter | solution.py:119
  523.5 29.1 %collective-permute-start = (bf16[8,2048]{1,0:T(8,128)(2,1)}, bf16[8,2048]{1,0:T(8,128)(2,1)S(1)}, u32[]{:S(2)}, u32[]{:S(2)}) collective-permute-start(bf16[8,2048]{1,0:T(8,128)(2,1)} %get-tuple-element.645), channel_id=1, source_target_pairs={{0,32},{16,48},{32,64},{48,80},{64,96},{80,112},{96,128},{112,144}... | collective-permute-start | bytes 98312 | tf_op jit(solution)/shard_map/while/body/eval_jaxpr/ppermute | solution.py:13
  650.6 125.9 %reduce-scatter.5.cloned.1.call-start = ((), (), s32[]{:S(2)}) async-start(), calls=%async_computation.3 | async-start | bytes 557056 | tf_op jit(solution)/shard_map/while/body/eval_jaxpr/reduce_scatter | solution.py:119
  650.6 29.1 %collective-permute-start = (bf16[8,2048]{1,0:T(8,128)(2,1)}, bf16[8,2048]{1,0:T(8,128)(2,1)S(1)}, u32[]{:S(2)}, u32[]{:S(2)}) collective-permute-start(bf16[8,2048]{1,0:T(8,128)(2,1)} %get-tuple-element.645), channel_id=1, source_target_pairs={{0,32},{16,48},{32,64},{48,80},{64,96},{80,112},{96,128},{112,144}... | collective-permute-start | bytes 98312 | tf_op jit(solution)/shard_map/while/body/eval_jaxpr/ppermute | solution.py:13
  778.9 126.0 %reduce-scatter.5.cloned.1.call-start = ((), (), s32[]{:S(2)}) async-start(), calls=%async_computation.3 | async-start | bytes 557056 | tf_op jit(solution)/shard_map/while/body/eval_jaxpr/reduce_scatter | solution.py:119
  778.9 29.1 %collective-permute-start = (bf16[8,2048]{1,0:T(8,128)(2,1)}, bf16[8,2048]{1,0:T(8,128)(2,1)S(1)}, u32[]{:S(2)}, u32[]{:S(2)}) collective-permute-start(bf16[8,2048]{1,0:T(8,128)(2,1)} %get-tuple-element.645), channel_id=1, source_target_pairs={{0,32},{16,48},{32,64},{48,80},{64,96},{80,112},{96,128},{112,144}... | collective-permute-start | bytes 98312 | tf_op jit(solution)/shard_map/while/body/eval_jaxpr/ppermute | solution.py:13
  907.2 126.0 %reduce-scatter.5.cloned.1.call-start = ((), (), s32[]{:S(2)}) async-start(), calls=%async_computation.3 | async-start | bytes 557056 | tf_op jit(solution)/shard_map/while/body/eval_jaxpr/reduce_scatter | solution.py:119
  907.3 29.1 %collective-permute-start = (bf16[8,2048]{1,0:T(8,128)(2,1)}, bf16[8,2048]{1,0:T(8,128)(2,1)S(1)}, u32[]{:S(2)}, u32[]{:S(2)}) collective-permute-start(bf16[8,2048]{1,0:T(8,128)(2,1)} %get-tuple-element.645), channel_id=1, source_target_pairs={{0,32},{16,48},{32,64},{48,80},{64,96},{80,112},{96,128},{112,144}... | collective-permute-start | bytes 98312 | tf_op jit(solution)/shard_map/while/body/eval_jaxpr/ppermute | solution.py:13
  1035.7 123.4 %reduce-scatter.5.cloned.1.call-start = ((), (), s32[]{:S(2)}) async-start(), calls=%async_computation.3 | async-start | bytes 557056 | tf_op jit(solution)/shard_map/while/body/eval_jaxpr/reduce_scatter | solution.py:119
  1035.7 29.1 %collective-permute-start = (bf16[8,2048]{1,0:T(8,128)(2,1)}, bf16[8,2048]{1,0:T(8,128)(2,1)S(1)}, u32[]{:S(2)}, u32[]{:S(2)}) collective-permute-start(bf16[8,2048]{1,0:T(8,128)(2,1)} %get-tuple-element.645), channel_id=1, source_target_pairs={{0,32},{16,48},{32,64},{48,80},{64,96},{80,112},{96,128},{112,144}... | collective-permute-start | bytes 98312 | tf_op jit(solution)/shard_map/while/body/eval_jaxpr/ppermute | solution.py:13
  1162.8 14.9 %collective-permute-start.1 = (bf16[1024,256]{1,0:T(8,128)(2,1)S(1)}, bf16[1024,256]{1,0:T(8,128)(2,1)S(1)}, u32[]{:S(2)}, u32[]{:S(2)}) collective-permute-start(bf16[1024,256]{1,0:T(8,128)(2,1)S(1)} %dynamic-slice_convert_fusion.2), channel_id=1, source_target_pairs={{0,16},{16,0},{32,48},{48,32},{64,80},{80,64},{96,112},{112,96},{1... | collective-permute-start | bytes 1572872 | tf_op jit(solution)/shard_map/ppermute | solution.py:23
  1164.6 24.3 %collective-permute-start.2 = (bf16[1024,256]{1,0:T(8,128)(2,1)S(1)}, bf16[1024,256]{1,0:T(8,128)(2,1)S(1)}, u32[]{:S(2)}, u32[]{:S(2)}) collective-permute-start(bf16[1024,256]{1,0:T(8,128)(2,1)S(1)} %dynamic-slice_convert_fusion.1), channel_id=1, source_target_pairs={{0,16},{16,0},{32,48},{48,32},{64,80},{80,64},{96,112},{112,96},{1... | collective-permute-start | bytes 1572872 | tf_op jit(solution)/shard_map/ppermute | solution.py:23
  1167.5 21.4 %copy-start.5 = (f32[1,1024,256]{2,1,0:T(8,128)S(1)}, f32[1,1024,256]{2,1,0:T(8,128)}, u32[]{:S(2)}) copy-start(f32[1,1024,256]{2,1,0:T(8,128)} %param.28) | copy-start | bytes 3145732
  1167.6 29.6 %collective-permute-start.3 = (bf16[256,1024]{1,0:T(8,128)(2,1)S(1)}, bf16[256,1024]{1,0:T(8,128)(2,1)S(1)}, u32[]{:S(2)}, u32[]{:S(2)}) collective-permute-start(bf16[256,1024]{1,0:T(8,128)(2,1)S(1)} %dynamic-slice_convert_fusion), channel_id=1, source_target_pairs={{0,16},{16,0},{32,48},{48,32},{64,80},{80,64},{96,112},{112,96},{1... | collective-permute-start | bytes 1572872 | tf_op jit(solution)/shard_map/ppermute | solution.py:23
  1180.0 17.1 %copy-start.6 = (f32[1,256,1024]{2,1,0:T(8,128)S(1)}, f32[1,256,1024]{2,1,0:T(8,128)}, u32[]{:S(2)}) copy-start(f32[1,256,1024]{2,1,0:T(8,128)} %param.29) | copy-start | bytes 3145732
  (7 other events, 30.4 us)
Sparse Core Ops, SparseCore 0:
  69.0 67.8 reduce-scatter.2
  195.5 69.7 reduce-scatter.4
  320.7 72.4 reduce-scatter.4
  448.6 72.4 reduce-scatter.4
  576.5 71.7 reduce-scatter.4
  703.6 72.8 reduce-scatter.4
  831.9 72.9 reduce-scatter.4
  960.2 73.0 reduce-scatter.4
  1088.7 70.3 reduce-scatter.4
where the time goes:
time: 1210 us
  waiting for transfers between devices  646 us (53%)
  blocking collectives  417 us (34%)
  starting transfers between devices  38.4 us (3%)
  other arithmetic  37.8 us (3%)
  matrix products  26.4 us (2%)
  local copies, waits for them, and re-layouts  25.8 us (2%)
  between operations  13.9 us (1%)
    reduce_scatter x9, waiting for transfers between devices, process(): lax.psum_scatter(lax.cond(active, compute, quiet).astype(jnp.bfloat16), '...  621 us
    all_gather x9, blocking collectives, process(): full_rows = lax.all_gather(normed[slot], 'tp', axis=0, tiled=True)  217 us
    all_gather x9, blocking collectives, process(): incoming_rows = lax.all_gather(local_in, 'tp', axis=0, tiled=True)  200 us
    ppermute x8, starting transfers between devices, passed_along(): return lax.ppermute(block, axis, route)  35.5 us
    ppermute x3, waiting for transfers between devices, partner(): return lax.ppermute(block, axis, route)  24.3 us
  transfers between devices with their start and end apart: 20, of which 12 were waited for; matrix products, arithmetic and copies ran while one was open for 3% of the time, Pallas kernels for 0%

commit v1 on v0

--- a/solution.py
+++ b/solution.py
@@ -96,7 +96,9 @@
         active = (index >= 0) & (index < micro)
         slot = jnp.clip(index, 0, micro - 1)
         local_in = jnp.where(position == 0, entry[slot], received)
-        incoming_rows = lax.all_gather(local_in, "tp", axis=0, tiled=True)
+        incoming_rows = jnp.concatenate(
+            lax.all_to_all(jnp.stack([local_in] * lax.axis_size("tp")), "tp", 0, 0), axis=0
+        )
         full_rows = lax.all_gather(normed[slot], "tp", axis=0, tiled=True)
 
         def factors():

time: 1210 us -> 1120 us (0.926)
  blocking collectives: 417 us -> 239 us
  starting transfers between devices: 38.4 us -> 83 us
  waiting for transfers between devices: 646 us -> 678 us
    all_gather x9 -> x0, blocking collectives: 200 us -> none  [process(): incoming_rows = lax.all_gather(local_in, 'tp', axis=0, tiled=True)]
    all_to_all x0 -> x9, starting transfers between devices: none -> 44.3 us  [process(): lax.all_to_all(jnp.stack([local_in] * lax.axis_size('tp')), 'tp', 0, 0)]
    all_gather x9, blocking collectives: 217 us -> 239 us  [process(): full_rows = lax.all_gather(normed[slot], 'tp', axis=0, tiled=True)]
    ppermute x8, waiting for transfers between devices: 0.02 us -> 16.1 us  [passed_along(): return lax.ppermute(block, axis, route)]
    reduce_scatter x9, waiting for transfers between devices: 621 us -> 637 us  [process(): lax.psum_scatter(lax.cond(active, compute, quiet).astype(jnp.bfloat16), '...]
  transfers between devices with their start and end apart: 20 -> 29, of which waited for: 12 -> 20; matrix products, arithmetic and copies ran while one was open for 3% -> 4% of each run, Pallas kernels for 0% -> 0%
where the time goes in v1:
time: 1120 us; the launch traced here: 1110 us
  waiting for transfers between devices  678 us (61%)
  blocking collectives  239 us (21%)
  starting transfers between devices  83 us (7%)
  other arithmetic  37.9 us (3%)
  local copies, waits for them, and re-layouts  34.8 us (3%)
  matrix products  22.6 us (2%)
  between operations  13.9 us (1%)
    reduce_scatter x9, waiting for transfers between devices, process(): lax.psum_scatter(lax.cond(active, compute, quiet).astype(jnp.bfloat16), '...  637 us
    all_gather x9, blocking collectives, process(): full_rows = lax.all_gather(normed[slot], 'tp', axis=0, tiled=True)  239 us
    all_to_all x9, starting transfers between devices, process(): lax.all_to_all(jnp.stack([local_in] * lax.axis_size('tp')), 'tp', 0, 0)  44.3 us
    ppermute x8, starting transfers between devices, passed_along(): return lax.ppermute(block, axis, route)  35.5 us
    ppermute x3, waiting for transfers between devices, partner(): return lax.ppermute(block, axis, route)  24.3 us
  transfers between devices with their start and end apart: 29, of which 20 were waited for; matrix products, arithmetic and copies ran while one was open for 4% of the time, Pallas kernels for 0%

profile of v1, /device:TPU:32, one launch (start us, length us, event | category | flops | bytes accessed | tf_op | source)
XLA Modules:
  0.0 1110.2 jit_solution(18129135491522319794)
XLA Ops:
  9.9 7.1 all-to-all-start.1
  19.4 26.5 %all-gather.1 = bf16[1,128,2048]{2,1,0:T(8,128)(2,1)S(1)} all-gather(bf16[1,8,2048]{2,1,0:T(8,128)(2,1)S(1)} %constant_dynamic-slice_fusion.3), channel_id=3, replica_groups=mesh['segment'=16,'tp'=16] {'tp'}, dimensions={1}, use_global_device_ids=true | all-gather | bytes 557056 | tf_op jit(solution)/shard_map/all_gather | solution.py:102
  52.0 6.4 conditional.8
  58.4 59.5 %reduce-scatter.3.cloned.1.call-done = bf16[8,2048]{1,0:T(8,128)(2,1)} async-done(((bf16[128,2048]{1,0:T(8,128)(2,1)}), bf16[8,2048]{1,0:T(8,128)(2,1)}) %reduce-scatter.3.cloned.1.call-update) | async-done | bytes 32784 | tf_op jit(solution)/shard_map/reduce_scatter | solution.py:121
  121.0 944.5 %while.22 = (s32[]{:T(128)}, bf16[8,2048]{1,0:T(8,128)(2,1)}, bf16[2,8,2048]{2,1,0:T(8,128)(2,1)}, f32[2048,256]{1,0:T(8,128)}, f32[2048,256]{1,0:T(8,128)}, /*i...) while((s32[]{:T(128)}, bf16[8,2048]{1,0:T(8,128)(2,1)}, ...), condition=%wide.region_18.19_spmd, body=%wide.region_9.18_spmd.sunk | while | flops 1076527104 | bytes 33882952 | solution.py:159
  134.5 26.6 %all-gather.3 = bf16[1,128,2048]{2,1,0:T(8,128)(2,1)S(1)} all-gather(bf16[1,8,2048]{2,1,0:T(8,128)(2,1)S(1)} %constant_dynamic-slice_fusion.8), channel_id=2, replica_groups=mesh['segment'=16,'tp'=16] {'tp'}, dimensions={1}, use_global_device_ids=true | all-gather | bytes 557056 | tf_op jit(solution)/shard_map/while/body/eval_jaxpr/all_gather | solution.py:102
  165.4 10.2 conditional.14
  175.6 59.8 %reduce-scatter.5.cloned.1.call-done = bf16[8,2048]{1,0:T(8,128)(2,1)} async-done(((bf16[128,2048]{1,0:T(8,128)(2,1)}), bf16[8,2048]{1,0:T(8,128)(2,1)}) %reduce-scatter.5.cloned.1.call-update) | async-done | bytes 32784 | tf_op jit(solution)/shard_map/while/body/eval_jaxpr/reduce_scatter | solution.py:121
  251.3 26.6 %all-gather.3 = bf16[1,128,2048]{2,1,0:T(8,128)(2,1)S(1)} all-gather(bf16[1,8,2048]{2,1,0:T(8,128)(2,1)S(1)} %constant_dynamic-slice_fusion.8), channel_id=2, replica_groups=mesh['segment'=16,'tp'=16] {'tp'}, dimensions={1}, use_global_device_ids=true | all-gather | bytes 557056 | tf_op jit(solution)/shard_map/while/body/eval_jaxpr/all_gather | solution.py:102
  279.7 75.2 %reduce-scatter.5.cloned.1.call-done = bf16[8,2048]{1,0:T(8,128)(2,1)} async-done(((bf16[128,2048]{1,0:T(8,128)(2,1)}), bf16[8,2048]{1,0:T(8,128)(2,1)}) %reduce-scatter.5.cloned.1.call-update) | async-done | bytes 32784 | tf_op jit(solution)/shard_map/while/body/eval_jaxpr/reduce_scatter | solution.py:121
  370.8 26.6 %all-gather.3 = bf16[1,128,2048]{2,1,0:T(8,128)(2,1)S(1)} all-gather(bf16[1,8,2048]{2,1,0:T(8,128)(2,1)S(1)} %constant_dynamic-slice_fusion.8), channel_id=2, replica_groups=mesh['segment'=16,'tp'=16] {'tp'}, dimensions={1}, use_global_device_ids=true | all-gather | bytes 557056 | tf_op jit(solution)/shard_map/while/body/eval_jaxpr/all_gather | solution.py:102
  399.1 75.2 %reduce-scatter.5.cloned.1.call-done = bf16[8,2048]{1,0:T(8,128)(2,1)} async-done(((bf16[128,2048]{1,0:T(8,128)(2,1)}), bf16[8,2048]{1,0:T(8,128)(2,1)}) %reduce-scatter.5.cloned.1.call-update) | async-done | bytes 32784 | tf_op jit(solution)/shard_map/while/body/eval_jaxpr/reduce_scatter | solution.py:121
  490.2 26.6 %all-gather.3 = bf16[1,128,2048]{2,1,0:T(8,128)(2,1)S(1)} all-gather(bf16[1,8,2048]{2,1,0:T(8,128)(2,1)S(1)} %constant_dynamic-slice_fusion.8), channel_id=2, replica_groups=mesh['segment'=16,'tp'=16] {'tp'}, dimensions={1}, use_global_device_ids=true | all-gather | bytes 557056 | tf_op jit(solution)/shard_map/while/body/eval_jaxpr/all_gather | solution.py:102
  518.5 72.6 %reduce-scatter.5.cloned.1.call-done = bf16[8,2048]{1,0:T(8,128)(2,1)} async-done(((bf16[128,2048]{1,0:T(8,128)(2,1)}), bf16[8,2048]{1,0:T(8,128)(2,1)}) %reduce-scatter.5.cloned.1.call-update) | async-done | bytes 32784 | tf_op jit(solution)/shard_map/while/body/eval_jaxpr/reduce_scatter | solution.py:121
  607.1 26.6 %all-gather.3 = bf16[1,128,2048]{2,1,0:T(8,128)(2,1)S(1)} all-gather(bf16[1,8,2048]{2,1,0:T(8,128)(2,1)S(1)} %constant_dynamic-slice_fusion.8), channel_id=2, replica_groups=mesh['segment'=16,'tp'=16] {'tp'}, dimensions={1}, use_global_device_ids=true | all-gather | bytes 557056 | tf_op jit(solution)/shard_map/while/body/eval_jaxpr/all_gather | solution.py:102
  635.4 72.6 %reduce-scatter.5.cloned.1.call-done = bf16[8,2048]{1,0:T(8,128)(2,1)} async-done(((bf16[128,2048]{1,0:T(8,128)(2,1)}), bf16[8,2048]{1,0:T(8,128)(2,1)}) %reduce-scatter.5.cloned.1.call-update) | async-done | bytes 32784 | tf_op jit(solution)/shard_map/while/body/eval_jaxpr/reduce_scatter | solution.py:121
  723.9 26.6 %all-gather.3 = bf16[1,128,2048]{2,1,0:T(8,128)(2,1)S(1)} all-gather(bf16[1,8,2048]{2,1,0:T(8,128)(2,1)S(1)} %constant_dynamic-slice_fusion.8), channel_id=2, replica_groups=mesh['segment'=16,'tp'=16] {'tp'}, dimensions={1}, use_global_device_ids=true | all-gather | bytes 557056 | tf_op jit(solution)/shard_map/while/body/eval_jaxpr/all_gather | solution.py:102
  752.2 74.9 %reduce-scatter.5.cloned.1.call-done = bf16[8,2048]{1,0:T(8,128)(2,1)} async-done(((bf16[128,2048]{1,0:T(8,128)(2,1)}), bf16[8,2048]{1,0:T(8,128)(2,1)}) %reduce-scatter.5.cloned.1.call-update) | async-done | bytes 32784 | tf_op jit(solution)/shard_map/while/body/eval_jaxpr/reduce_scatter | solution.py:121
  843.1 26.6 %all-gather.3 = bf16[1,128,2048]{2,1,0:T(8,128)(2,1)S(1)} all-gather(bf16[1,8,2048]{2,1,0:T(8,128)(2,1)S(1)} %constant_dynamic-slice_fusion.8), channel_id=2, replica_groups=mesh['segment'=16,'tp'=16] {'tp'}, dimensions={1}, use_global_device_ids=true | all-gather | bytes 557056 | tf_op jit(solution)/shard_map/while/body/eval_jaxpr/all_gather | solution.py:102
  871.4 74.9 %reduce-scatter.5.cloned.1.call-done = bf16[8,2048]{1,0:T(8,128)(2,1)} async-done(((bf16[128,2048]{1,0:T(8,128)(2,1)}), bf16[8,2048]{1,0:T(8,128)(2,1)}) %reduce-scatter.5.cloned.1.call-update) | async-done | bytes 32784 | tf_op jit(solution)/shard_map/while/body/eval_jaxpr/reduce_scatter | solution.py:121
  962.2 26.6 %all-gather.3 = bf16[1,128,2048]{2,1,0:T(8,128)(2,1)S(1)} all-gather(bf16[1,8,2048]{2,1,0:T(8,128)(2,1)S(1)} %constant_dynamic-slice_fusion.8), channel_id=2, replica_groups=mesh['segment'=16,'tp'=16] {'tp'}, dimensions={1}, use_global_device_ids=true | all-gather | bytes 557056 | tf_op jit(solution)/shard_map/while/body/eval_jaxpr/all_gather | solution.py:102
  990.5 72.6 %reduce-scatter.5.cloned.1.call-done = bf16[8,2048]{1,0:T(8,128)(2,1)} async-done(((bf16[128,2048]{1,0:T(8,128)(2,1)}), bf16[8,2048]{1,0:T(8,128)(2,1)}) %reduce-scatter.5.cloned.1.call-update) | async-done | bytes 32784 | tf_op jit(solution)/shard_map/while/body/eval_jaxpr/reduce_scatter | solution.py:121
  1072.2 9.6 collective-permute-done.1
  1084.1 8.9 collective-permute-done.2
  (224 shorter events, 207.0 us)
Async XLA Ops:
  9.9 36.0 %all-to-all-start.1 = ((bf16[16,8,2048]{2,1,0:T(8,128)(2,1)}), bf16[16,8,2048]{2,1,0:T(8,128)(2,1)}, u32[]{:S(2)}, u32[]{:S(2)}) async-start(bf16[16,8,2048]{2,1,0:T(8,128)(2,1)} %stack.8), calls=%async_computation.2 | async-start | bytes 1048576 | tf_op jit(solution)/shard_map/all_to_all | solution.py:100
  17.0 100.9 %reduce-scatter.3.cloned.1.call-start = ((), (), s32[]{:S(2)}) async-start(), calls=%async_computation.4 | async-start | bytes 557056 | tf_op jit(solution)/shard_map/reduce_scatter | solution.py:121
  121.0 6.5 collective-permute-start
  129.1 32.0 %all-to-all-start = ((bf16[16,8,2048]{2,1,0:T(8,128)(2,1)}), bf16[16,8,2048]{2,1,0:T(8,128)(2,1)S(1)}, u32[]{:S(2)}, u32[]{:S(2)}) async-start(bf16[16,8,2048]{2,1,0:T(8,128)(2,1)} %stack.10), calls=%async_computation | async-start | bytes 1048576 | tf_op jit(solution)/shard_map/while/body/eval_jaxpr/all_to_all | solution.py:100
  133.7 101.7 %reduce-scatter.5.cloned.1.call-start = ((), (), s32[]{:S(2)}) async-start(), calls=%async_computation.5 | async-start | bytes 557056 | tf_op jit(solution)/shard_map/while/body/eval_jaxpr/reduce_scatter | solution.py:121
  237.8 6.5 collective-permute-start
  245.9 32.0 %all-to-all-start = ((bf16[16,8,2048]{2,1,0:T(8,128)(2,1)}), bf16[16,8,2048]{2,1,0:T(8,128)(2,1)S(1)}, u32[]{:S(2)}, u32[]{:S(2)}) async-start(bf16[16,8,2048]{2,1,0:T(8,128)(2,1)} %stack.10), calls=%async_computation | async-start | bytes 1048576 | tf_op jit(solution)/shard_map/while/body/eval_jaxpr/all_to_all | solution.py:100
  250.5 104.3 %reduce-scatter.5.cloned.1.call-start = ((), (), s32[]{:S(2)}) async-start(), calls=%async_computation.5 | async-start | bytes 557056 | tf_op jit(solution)/shard_map/while/body/eval_jaxpr/reduce_scatter | solution.py:121
  365.3 32.1 %all-to-all-start = ((bf16[16,8,2048]{2,1,0:T(8,128)(2,1)}), bf16[16,8,2048]{2,1,0:T(8,128)(2,1)S(1)}, u32[]{:S(2)}, u32[]{:S(2)}) async-start(bf16[16,8,2048]{2,1,0:T(8,128)(2,1)} %stack.10), calls=%async_computation | async-start | bytes 1048576 | tf_op jit(solution)/shard_map/while/body/eval_jaxpr/all_to_all | solution.py:100
  370.0 104.3 %reduce-scatter.5.cloned.1.call-start = ((), (), s32[]{:S(2)}) async-start(), calls=%async_computation.5 | async-start | bytes 557056 | tf_op jit(solution)/shard_map/while/body/eval_jaxpr/reduce_scatter | solution.py:121
  484.7 32.1 %all-to-all-start = ((bf16[16,8,2048]{2,1,0:T(8,128)(2,1)}), bf16[16,8,2048]{2,1,0:T(8,128)(2,1)S(1)}, u32[]{:S(2)}, u32[]{:S(2)}) async-start(bf16[16,8,2048]{2,1,0:T(8,128)(2,1)} %stack.10), calls=%async_computation | async-start | bytes 1048576 | tf_op jit(solution)/shard_map/while/body/eval_jaxpr/all_to_all | solution.py:100
  489.4 101.8 %reduce-scatter.5.cloned.1.call-start = ((), (), s32[]{:S(2)}) async-start(), calls=%async_computation.5 | async-start | bytes 557056 | tf_op jit(solution)/shard_map/while/body/eval_jaxpr/reduce_scatter | solution.py:121
  593.5 6.5 collective-permute-start
  601.6 32.1 %all-to-all-start = ((bf16[16,8,2048]{2,1,0:T(8,128)(2,1)}), bf16[16,8,2048]{2,1,0:T(8,128)(2,1)S(1)}, u32[]{:S(2)}, u32[]{:S(2)}) async-start(bf16[16,8,2048]{2,1,0:T(8,128)(2,1)} %stack.10), calls=%async_computation | async-start | bytes 1048576 | tf_op jit(solution)/shard_map/while/body/eval_jaxpr/all_to_all | solution.py:100
  606.3 101.7 %reduce-scatter.5.cloned.1.call-start = ((), (), s32[]{:S(2)}) async-start(), calls=%async_computation.5 | async-start | bytes 557056 | tf_op jit(solution)/shard_map/while/body/eval_jaxpr/reduce_scatter | solution.py:121
  718.4 32.1 %all-to-all-start = ((bf16[16,8,2048]{2,1,0:T(8,128)(2,1)}), bf16[16,8,2048]{2,1,0:T(8,128)(2,1)S(1)}, u32[]{:S(2)}, u32[]{:S(2)}) async-start(bf16[16,8,2048]{2,1,0:T(8,128)(2,1)} %stack.10), calls=%async_computation | async-start | bytes 1048576 | tf_op jit(solution)/shard_map/while/body/eval_jaxpr/all_to_all | solution.py:100
  723.1 104.0 %reduce-scatter.5.cloned.1.call-start = ((), (), s32[]{:S(2)}) async-start(), calls=%async_computation.5 | async-start | bytes 557056 | tf_op jit(solution)/shard_map/while/body/eval_jaxpr/reduce_scatter | solution.py:121
  837.5 32.1 %all-to-all-start = ((bf16[16,8,2048]{2,1,0:T(8,128)(2,1)}), bf16[16,8,2048]{2,1,0:T(8,128)(2,1)S(1)}, u32[]{:S(2)}, u32[]{:S(2)}) async-start(bf16[16,8,2048]{2,1,0:T(8,128)(2,1)} %stack.10), calls=%async_computation | async-start | bytes 1048576 | tf_op jit(solution)/shard_map/while/body/eval_jaxpr/all_to_all | solution.py:100
  842.2 104.0 %reduce-scatter.5.cloned.1.call-start = ((), (), s32[]{:S(2)}) async-start(), calls=%async_computation.5 | async-start | bytes 557056 | tf_op jit(solution)/shard_map/while/body/eval_jaxpr/reduce_scatter | solution.py:121
  956.7 32.1 %all-to-all-start = ((bf16[16,8,2048]{2,1,0:T(8,128)(2,1)}), bf16[16,8,2048]{2,1,0:T(8,128)(2,1)S(1)}, u32[]{:S(2)}, u32[]{:S(2)}) async-start(bf16[16,8,2048]{2,1,0:T(8,128)(2,1)} %stack.10), calls=%async_computation | async-start | bytes 1048576 | tf_op jit(solution)/shard_map/while/body/eval_jaxpr/all_to_all | solution.py:100
  961.4 101.7 %reduce-scatter.5.cloned.1.call-start = ((), (), s32[]{:S(2)}) async-start(), calls=%async_computation.5 | async-start | bytes 557056 | tf_op jit(solution)/shard_map/while/body/eval_jaxpr/reduce_scatter | solution.py:121
  1066.8 15.0 %collective-permute-start.1 = (bf16[1024,256]{1,0:T(8,128)(2,1)S(1)}, bf16[1024,256]{1,0:T(8,128)(2,1)S(1)}, u32[]{:S(2)}, u32[]{:S(2)}) collective-permute-start(bf16[1024,256]{1,0:T(8,128)(2,1)S(1)} %dynamic-slice_convert_fusion.2), channel_id=1, source_target_pairs={{0,16},{16,0},{32,48},{48,32},{64,80},{80,64},{96,112},{112,96},{1... | collective-permute-start | bytes 1572872 | tf_op jit(solution)/shard_map/ppermute | solution.py:23
  1068.7 24.3 %collective-permute-start.2 = (bf16[1024,256]{1,0:T(8,128)(2,1)S(1)}, bf16[1024,256]{1,0:T(8,128)(2,1)S(1)}, u32[]{:S(2)}, u32[]{:S(2)}) collective-permute-start(bf16[1024,256]{1,0:T(8,128)(2,1)S(1)} %dynamic-slice_convert_fusion.1), channel_id=1, source_target_pairs={{0,16},{16,0},{32,48},{48,32},{64,80},{80,64},{96,112},{112,96},{1... | collective-permute-start | bytes 1572872 | tf_op jit(solution)/shard_map/ppermute | solution.py:23
  1071.6 29.6 %collective-permute-start.3 = (bf16[256,1024]{1,0:T(8,128)(2,1)S(1)}, bf16[256,1024]{1,0:T(8,128)(2,1)S(1)}, u32[]{:S(2)}, u32[]{:S(2)}) collective-permute-start(bf16[256,1024]{1,0:T(8,128)(2,1)S(1)} %dynamic-slice_convert_fusion), channel_id=1, source_target_pairs={{0,16},{16,0},{32,48},{48,32},{64,80},{80,64},{96,112},{112,96},{1... | collective-permute-start | bytes 1572872 | tf_op jit(solution)/shard_map/ppermute | solution.py:23
  (14 other events, 168.5 us)
Sparse Core Ops, SparseCore 0:
  50.6 67.2 reduce-scatter.2
  164.8 70.6 reduce-scatter.4
  279.0 75.8 reduce-scatter.4
  398.4 75.7 reduce-scatter.4
  517.9 73.2 reduce-scatter.4
  634.7 73.1 reduce-scatter.4
  751.5 75.5 reduce-scatter.4
  870.7 75.5 reduce-scatter.4
  989.9 73.2 reduce-scatter.4
